TPU v7x, 256 devices: a whole 4x4x8 slice. The times are simulated.
256 devices in a mesh: row: 4 (over y), col: 16 (over z, core), layer: 4 (over x).
Axes of the slice: x: 4, y: 4, z: 8, core: 2. Of those that a mesh axis runs over, the one named last changes fastest.
Arguments:
- density: float32 [4096, 4096], P('row', 'col'), may hold values from -1 to 1, as said below
- pattern: int32 [64, 64], replicated, may hold values from 0 to 1, as said below
Outputs:
- purified: float32 [4096, 4096], P('row', 'col')
- traces: float32 [2], replicated
Inputs may be any that keep to these rules, and one draw needn't show every extreme that they name: pattern is symmetric and is 1 on the block diagonal and next to it. density is symmetric and zero outside the blocks that pattern keeps.
All inputs are finite; a program needn't handle non-finite values.
Results may differ from a plain program's by a relative error of at most 0.0003.
Values sent between devices are 32-bit elements; how exact they have to be, the bound alone decides.
No kernel may reach another device: no remote copies, remote signals or barrier semaphores. Data moves between devices by JAX's collectives and lax.ppermute only.
A program may use at most 64 MiB of HBM per device.

v0:
```python
import jax
import jax.numpy as jnp
from jax import lax
from jax.sharding import PartitionSpec as P

BS = 64
STEPS = 2
HIGHEST = lax.Precision.HIGHEST


def pick_columns(tile, layer_index, unit_width, layers):
    tile_rows, tile_cols = tile.shape
    shaped = tile.reshape(tile_rows, tile_cols // (layers * unit_width), layers, unit_width)
    picked = lax.dynamic_index_in_dim(shaped, layer_index, 2, keepdims=False)
    return picked.reshape(tile_rows, tile_cols // layers)


def pick_rows(tile, layer_index, unit_width, layers):
    tile_rows, tile_cols = tile.shape
    shaped = tile.reshape(tile_rows // (layers * unit_width), layers, unit_width, tile_cols)
    picked = lax.dynamic_index_in_dim(shaped, layer_index, 1, keepdims=False)
    return picked.reshape(tile_rows // layers, tile_cols)


def reduce_layers(layer_term):
    summed = lax.psum(layer_term, "layer")
    return summed


def right_panel(right, layer_index, unit_width, layers):
    return lax.all_gather(
        pick_rows(right, layer_index, unit_width, layers), "row", axis=0, tiled=True
    )


def folded_product(left, right, layer_index, unit_width, layers, occupied):
    tall_panel = right_panel(right, layer_index, unit_width, layers)
    layer_term = jnp.dot(
        lax.all_gather(
            pick_columns(left, layer_index, unit_width, layers), "col", axis=1, tiled=True
        ),
        tall_panel,
        precision=HIGHEST,
        preferred_element_type=jnp.float32,
    )
    summed = reduce_layers(layer_term)
    return jnp.where(occupied, summed, jnp.zeros_like(summed))


def body(density, pattern):
    tile_rows, tile_cols = density.shape
    layers = lax.axis_size("layer")
    unit_width = tile_cols // (lax.axis_size("row") * layers)
    layer_index = lax.axis_index("layer")
    row_ids = lax.axis_index("row") * tile_rows + jnp.arange(tile_rows, dtype=jnp.int32)
    col_ids = lax.axis_index("col") * tile_cols + jnp.arange(tile_cols, dtype=jnp.int32)
    blocks = jnp.arange(pattern.shape[0], dtype=jnp.int32)
    row_onehot = (row_ids[:, None] // BS == blocks[None, :]).astype(jnp.bfloat16)
    col_onehot = (blocks[:, None] == col_ids[None, :] // BS).astype(jnp.bfloat16)
    row_pattern = jnp.dot(
        row_onehot, pattern.astype(jnp.bfloat16), preferred_element_type=jnp.float32
    )
    occupied = (
        jnp.dot(row_pattern.astype(jnp.bfloat16), col_onehot, preferred_element_type=jnp.float32)
        > 0.5
    )
    on_diag = row_ids[:, None] == col_ids[None, :]
    current = density
    trace_list = []
    for iteration in range(STEPS):
        square = folded_product(current, current, layer_index, unit_width, layers, occupied)
        cube_term = folded_product(current, square, layer_index, unit_width, layers, occupied)
        current = 3.0 * square - 2.0 * cube_term
        diag_part = jnp.sum(jnp.where(on_diag, current, jnp.zeros_like(current)))
        trace_list.append(lax.psum(diag_part, ("row", "col")))
    stacked = jnp.stack(trace_list)
    return (current, stacked)


def solution(mesh):
    placed = (P("row", "col"), P())
    return jax.shard_map(
        body, mesh=mesh, in_specs=placed, out_specs=(P("row", "col"), P()), check_vma=False
    )
```

profile of v0, /device:TPU:2, one launch (start us, length us, event | category | flops | bytes accessed | tf_op | source)
XLA Modules:
  0.0 601.4 jit_solution(12206215405275679510)
XLA Ops:
  7.2 0.0 all-gather.9.cloned.1.call-start
  7.2 1.7 constant_dynamic-slice_fusion.4
  8.9 0.0 all-gather.9.cloned.1.call-update
  8.9 0.0 all-gather.7.cloned.1.call-start
  9.0 1.6 copy.4
  10.6 0.0 copy-start.2
  10.6 0.7 constant_dynamic-slice_fusion.5
  11.3 0.0 all-gather.7.cloned.1.call-update
  11.3 0.0 all-reduce.6.cloned.1.call-start
  11.4 28.0 %all-gather.9.cloned.1.call-done = f32[1024,256]{1,0:T(8,128)} async-done(((f32[256,256]{1,0:T(8,128)}), f32[1024,256]{1,0:T(8,128)}) %all-gather.9.cloned.1.call-update) | async-done | bytes 1048592 | tf_op jit(solution)/shard_map/all_gather | solution.py:31
  39.3 44.9 %all-gather.7.cloned.1.call-done = f32[1024,1024]{0,1:T(8,128)} async-done(((f32[1024,64]{0,1:T(8,128)}), f32[1024,1024]{0,1:T(8,128)}) %all-gather.7.cloned.1.call-update) | async-done | bytes 4194320 | tf_op jit(solution)/shard_map/all_gather | solution.py:39
  84.2 10.1 %fusion.12 = f32[1024,256]{1,0:T(8,128)} fusion(f32[1024,1024]{0,1:T(8,128)} %all-gather.7.cloned.1.call-done, f32[1024,256]{1,0:T(8,128)} %all-gather.9.cloned.1.call-done), kind=kOutput, calls=%fused_computation.36 | convolution fusion | flops 3221225472 | bytes 6291456 | tf_op jit(solution)/shard_map/dot_general | solution.py:38
  94.3 0.0 all-reduce.6.cloned.1.call-update
  94.4 0.0 all-gather.11.cloned.1.call-start
  94.4 48.7 %all-reduce.6.cloned.1.call-done = f32[1024,256]{1,0:T(8,128)} async-done(((f32[1024,256]{1,0:T(8,128)}), f32[1024,256]{1,0:T(8,128)}) %all-reduce.6.cloned.1.call-update) | async-done | bytes 1048592 | tf_op jit(solution)/shard_map/psum | solution.py:26
  143.2 0.0 copy-done.2
  143.2 1.8 broadcast_select_fusion.1
  145.0 0.0 copy-start.1
  145.0 0.7 constant_dynamic-slice_fusion.3
  145.7 0.0 all-gather.11.cloned.1.call-update
  145.7 0.2 all-reduce.8.cloned.1.call-start
  146.0 28.2 %all-gather.11.cloned.1.call-done = f32[1024,256]{1,0:T(8,128)} async-done(((f32[256,256]{1,0:T(8,128)}), f32[1024,256]{1,0:T(8,128)}) %all-gather.11.cloned.1.call-update) | async-done | bytes 1048592 | tf_op jit(solution)/shard_map/all_gather | solution.py:31
  174.1 10.1 %fusion.13 = f32[1024,256]{1,0:T(8,128)} fusion(f32[1024,1024]{0,1:T(8,128)} %all-gather.7.cloned.1.call-done, f32[1024,256]{1,0:T(8,128)} %all-gather.11.cloned.1.call-done), kind=kOutput, calls=%fused_computation.37 | convolution fusion | flops 3221225472 | bytes 6291456 | tf_op jit(solution)/shard_map/dot_general | solution.py:38
  184.2 0.0 all-reduce.8.cloned.1.call-update
  184.3 0.0 all-gather.15.cloned.1.call-start
  184.3 50.6 %all-reduce.8.cloned.1.call-done = f32[1024,256]{1,0:T(8,128)} async-done(((f32[1024,256]{1,0:T(8,128)}), f32[1024,256]{1,0:T(8,128)}) %all-reduce.8.cloned.1.call-update) | async-done | bytes 1048592 | tf_op jit(solution)/shard_map/psum | solution.py:26
  234.9 0.0 copy-done.1
  234.9 1.5 multiply_subtract_fusion.1
  236.3 0.8 constant_dynamic-slice_fusion.1
  237.1 0.0 all-gather.15.cloned.1.call-update
  237.1 0.0 all-gather.13.cloned.1.call-start
  237.2 0.3 copy.5
  237.5 0.7 constant_dynamic-slice_fusion.2
  238.2 0.0 all-gather.13.cloned.1.call-update
  238.2 0.3 all-reduce.10.cloned.1.call-start
  238.5 27.0 %all-gather.15.cloned.1.call-done = f32[1024,256]{1,0:T(8,128)} async-done(((f32[256,256]{1,0:T(8,128)}), f32[1024,256]{1,0:T(8,128)}) %all-gather.15.cloned.1.call-update) | async-done | bytes 1048592 | tf_op jit(solution)/shard_map/all_gather | solution.py:31
  265.5 44.9 %all-gather.13.cloned.1.call-done = f32[1024,1024]{0,1:T(8,128)} async-done(((f32[1024,64]{0,1:T(8,128)}), f32[1024,1024]{0,1:T(8,128)}) %all-gather.13.cloned.1.call-update) | async-done | bytes 4194320 | tf_op jit(solution)/shard_map/all_gather | solution.py:39
  310.4 10.1 %fusion.14 = f32[1024,256]{1,0:T(8,128)} fusion(f32[1024,1024]{0,1:T(8,128)} %all-gather.13.cloned.1.call-done, f32[1024,256]{1,0:T(8,128)} %all-gather.15.cloned.1.call-done), kind=kOutput, calls=%fused_computation.38 | convolution fusion | flops 3221225472 | bytes 6291456 | tf_op jit(solution)/shard_map/dot_general | solution.py:38
  320.5 0.0 all-reduce.10.cloned.1.call-update
  320.5 0.0 all-gather.17.cloned.1.call-start
  320.5 48.8 %all-reduce.10.cloned.1.call-done = f32[1024,256]{1,0:T(8,128)} async-done(((f32[1024,256]{1,0:T(8,128)}), f32[1024,256]{1,0:T(8,128)}) %all-reduce.10.cloned.1.call-update) | async-done | bytes 1048592 | tf_op jit(solution)/shard_map/psum | solution.py:26
  369.3 1.3 broadcast_select_fusion
  370.7 0.0 copy-start
  370.7 0.7 constant_dynamic-slice_fusion
  371.4 0.0 all-gather.17.cloned.1.call-update
  371.4 0.3 all-reduce.12.cloned.1.call-start
  371.8 28.4 %all-gather.17.cloned.1.call-done = f32[1024,256]{1,0:T(8,128)} async-done(((f32[256,256]{1,0:T(8,128)}), f32[1024,256]{1,0:T(8,128)}) %all-gather.17.cloned.1.call-update) | async-done | bytes 1048592 | tf_op jit(solution)/shard_map/all_gather | solution.py:31
  400.1 10.1 %fusion.15 = f32[1024,256]{1,0:T(8,128)} fusion(f32[1024,1024]{0,1:T(8,128)} %all-gather.13.cloned.1.call-done, f32[1024,256]{1,0:T(8,128)} %all-gather.17.cloned.1.call-done), kind=kOutput, calls=%fused_computation.39 | convolution fusion | flops 3221225472 | bytes 6291456 | tf_op jit(solution)/shard_map/dot_general | solution.py:38
  410.2 0.0 all-reduce.12.cloned.1.call-update
  410.3 50.6 %all-reduce.12.cloned.1.call-done = f32[1024,256]{1,0:T(8,128)} async-done(((f32[1024,256]{1,0:T(8,128)}), f32[1024,256]{1,0:T(8,128)}) %all-reduce.12.cloned.1.call-update) | async-done | bytes 1048592 | tf_op jit(solution)/shard_map/psum | solution.py:26
  460.9 0.0 copy-done
  460.9 3.2 fusion
  464.1 128.6 %all-reduce = (f32[1]{0:T(128)}, f32[1]{0:T(128)}) all-reduce(f32[1]{0:T(128)} %bitcast.13, f32[1]{0:T(128)} %bitcast.12), channel_id=1, replica_groups=mesh['row'=4,'col'=16,'layer'=4] {'row','col'}, use_global_device_ids=true, to_apply=%region_7.8 | all-reduce | flops 2 | bytes 16 | tf_op jit(solution)/shard_map/psum | solution.py:75
  592.7 1.8 pad_maximum_fusion
  (4 shorter events, 0.0 us)
Async XLA Ops:
  7.2 32.2 %all-gather.9.cloned.1.call-start = ((), (), s32[]{:S(2)}) async-start(), calls=%async_computation.1 | async-start | bytes 1310720 | tf_op jit(solution)/shard_map/all_gather | solution.py:31
  8.9 75.3 %all-gather.7.cloned.1.call-start = ((), (), s32[]{:S(2)}) async-start(), calls=%async_computation | async-start | bytes 4456448 | tf_op jit(solution)/shard_map/all_gather | solution.py:39
  10.6 132.6 %copy-start.2 = (s32[64,64]{1,0:T(8,128)S(1)}, s32[64,64]{1,0:T(8,128)}, u32[]{:S(2)}) copy-start(s32[64,64]{1,0:T(8,128)} %param.3) | copy-start | bytes 49156
  11.3 131.9 %all-reduce.6.cloned.1.call-start = ((), (), s32[]{:S(2)}) async-start(), calls=%async_computation.2 | async-start | bytes 2097152 | tf_op jit(solution)/shard_map/psum | solution.py:26
  94.4 79.8 %all-gather.11.cloned.1.call-start = ((), (), s32[]{:S(2)}) async-start(), calls=%async_computation.3 | async-start | bytes 1310720 | tf_op jit(solution)/shard_map/all_gather | solution.py:31
  145.0 89.9 %copy-start.1 = (f32[1024,256]{1,0:T(8,128)S(1)}, f32[1024,256]{1,0:T(8,128)}, u32[]{:S(2)}) copy-start(f32[1024,256]{1,0:T(8,128)} %all-reduce.6.cloned.1.call-done) | copy-start | bytes 3145732
  145.7 89.1 %all-reduce.8.cloned.1.call-start = ((), (), s32[]{:S(2)}) async-start(), calls=%async_computation.4 | async-start | bytes 2097152 | tf_op jit(solution)/shard_map/psum | solution.py:26
  184.3 81.2 %all-gather.15.cloned.1.call-start = ((), (), s32[]{:S(2)}) async-start(), calls=%async_computation.6 | async-start | bytes 1310720 | tf_op jit(solution)/shard_map/all_gather | solution.py:31
  237.1 73.2 %all-gather.13.cloned.1.call-start = ((), (), s32[]{:S(2)}) async-start(), calls=%async_computation.5 | async-start | bytes 4456448 | tf_op jit(solution)/shard_map/all_gather | solution.py:39
  238.2 131.1 %all-reduce.10.cloned.1.call-start = ((), (), s32[]{:S(2)}) async-start(), calls=%async_computation.7 | async-start | bytes 2097152 | tf_op jit(solution)/shard_map/psum | solution.py:26
  320.5 79.6 %all-gather.17.cloned.1.call-start = ((), (), s32[]{:S(2)}) async-start(), calls=%async_computation.8 | async-start | bytes 1310720 | tf_op jit(solution)/shard_map/all_gather | solution.py:31
  370.7 90.2 %copy-start = (f32[1024,256]{1,0:T(8,128)S(1)}, f32[1024,256]{1,0:T(8,128)}, u32[]{:S(2)}) copy-start(f32[1024,256]{1,0:T(8,128)} %all-reduce.10.cloned.1.call-done) | copy-start | bytes 3145732
  371.4 89.4 %all-reduce.12.cloned.1.call-start = ((), (), s32[]{:S(2)}) async-start(), calls=%async_computation.9 | async-start | bytes 2097152 | tf_op jit(solution)/shard_map/psum | solution.py:26
Sparse Core Ops, SparseCore 0:
  9.8 29.4 all-gather.8
  41.7 42.4 all-gather.6
  94.5 48.6 all-reduce.5
  145.8 28.2 all-gather.10
  184.4 50.4 all-reduce.7
  237.2 28.2 all-gather.14
  267.9 42.4 all-gather.12
  320.6 48.6 all-reduce.9
  371.9 28.2 all-gather.16
  410.4 50.4 all-reduce.11
where the time goes:
time: 602 us; the launch traced here: 601 us
  waiting for transfers between devices  400 us (66%)
  blocking collectives  129 us (21%)
  matrix products  42.3 us (7%)
  between operations  14.3 us (2%)
  other arithmetic  7.89 us (1%)
  local copies, waits for them, and re-layouts  7.27 us (1%)
    psum x4, waiting for transfers between devices, reduce_layers(): summed = lax.psum(layer_term, 'layer')  199 us
    psum x1, blocking collectives, body(): trace_list.append(lax.psum(diag_part, ('row', 'col')))  129 us
    all_gather x4, waiting for transfers between devices, right_panel(): lax.all_gather(pick_rows(right, layer_index, unit_width, layers), 'row',...  111 us
    all_gather x2, waiting for transfers between devices, folded_product(): lax.all_gather(pick_columns(left, layer_index, unit_width, layers), 'col'...  89.7 us
    dot_general x4, matrix products, folded_product(): jnp.dot(lax.all_gather(pick_columns(left, layer_index, unit_width, layers...  40.5 us
  transfers between devices with their start and end apart: 10, of which 10 were waited for; matrix products, arithmetic and copies ran while one was open for 1% of the time, Pallas kernels for 0%

commit v1 on v0

--- a/solution.py
+++ b/solution.py
@@ -23,7 +23,8 @@
 
 
 def reduce_layers(layer_term):
-    summed = lax.psum(layer_term, "layer")
+    pieces = lax.all_gather(layer_term, "layer")
+    summed = jnp.sum(pieces, axis=0)
     return summed
 
 

time: 602 us -> 606 us (level)
  other arithmetic: 7.89 us -> 14.6 us
    all_gather x0 -> x4, waiting for transfers between devices: none -> 199 us  [reduce_layers(): pieces = lax.all_gather(layer_term, 'layer')]
    psum x4 -> x0, waiting for transfers between devices: 199 us -> none  [reduce_layers(): summed = lax.psum(layer_term, 'layer')]
    reduce_sum x0 -> x4, other arithmetic: none -> 10.4 us  [reduce_layers(): summed = jnp.sum(pieces, axis=0)]
where the time goes in v1:
time: 606 us
  waiting for transfers between devices  398 us (66%)
  blocking collectives  130 us (21%)
  matrix products  41 us (7%)
  other arithmetic  14.6 us (2%)
  between operations  14.3 us (2%)
  local copies, waits for them, and re-layouts  7.25 us (1%)
    all_gather x4, waiting for transfers between devices, reduce_layers(): pieces = lax.all_gather(layer_term, 'layer')  199 us
    psum x1, blocking collectives, body(): trace_list.append(lax.psum(diag_part, ('row', 'col')))  130 us
    all_gather x4, waiting for transfers between devices, right_panel(): lax.all_gather(pick_rows(right, layer_index, unit_width, layers), 'row',...  109 us
    all_gather x2, waiting for transfers between devices, folded_product(): lax.all_gather(pick_columns(left, layer_index, unit_width, layers), 'col'...  89.7 us
    dot_general x4, matrix products, folded_product(): jnp.dot(lax.all_gather(pick_columns(left, layer_index, unit_width, layers...  40.5 us
  transfers between devices with their start and end apart: 10, of which 10 were waited for; matrix products, arithmetic and copies ran while one was open for 1% of the time, Pallas kernels for 0%

profile of v1, /device:TPU:2, one launch (start us, length us, event | category | flops | bytes accessed | tf_op | source)
XLA Modules:
  0.0 605.8 jit_solution(403896020922950800)
XLA Ops:
  7.2 0.0 all-gather.17.cloned.1.call-start
  7.2 1.7 constant_dynamic-slice_fusion.4
  8.9 0.0 all-gather.17.cloned.1.call-update
  8.9 0.0 all-gather.15.cloned.1.call-start
  9.0 1.6 copy.4
  10.5 0.7 constant_dynamic-slice_fusion.5
  11.3 0.0 all-gather.15.cloned.1.call-update
  11.3 0.0 all-gather.27.cloned.1.call-start
  11.3 28.0 %all-gather.17.cloned.1.call-done = f32[1024,256]{1,0:T(8,128)} async-done(((f32[256,256]{1,0:T(8,128)}), f32[1024,256]{1,0:T(8,128)}) %all-gather.17.cloned.1.call-update) | async-done | bytes 1048592 | tf_op jit(solution)/shard_map/all_gather | solution.py:32
  39.3 44.9 %all-gather.15.cloned.1.call-done = f32[1024,1024]{0,1:T(8,128)} async-done(((f32[1024,64]{0,1:T(8,128)}), f32[1024,1024]{0,1:T(8,128)}) %all-gather.15.cloned.1.call-update) | async-done | bytes 4194320 | tf_op jit(solution)/shard_map/all_gather | solution.py:40
  84.2 10.1 %fusion.12 = f32[1024,256]{1,0:T(8,128)} fusion(f32[1024,1024]{0,1:T(8,128)} %all-gather.15.cloned.1.call-done, f32[1024,256]{1,0:T(8,128)} %all-gather.17.cloned.1.call-done), kind=kOutput, calls=%fused_computation.36 | convolution fusion | flops 3221225472 | bytes 6291456 | tf_op jit(solution)/shard_map/dot_general | solution.py:39
  94.3 0.0 copy-start
  94.3 0.0 all-gather.27.cloned.1.call-update
  94.4 0.0 all-gather.19.cloned.1.call-start
  94.4 48.8 %all-gather.27.cloned.1.call-done = f32[4096,256]{1,0:T(8,128)} async-done(((f32[1024,256]{1,0:T(8,128)}), f32[4096,256]{1,0:T(8,128)}) %all-gather.27.cloned.1.call-update) | async-done | bytes 4194320 | tf_op jit(solution)/shard_map/all_gather | solution.py:26
  143.3 2.6 reduce_sum.54
  145.9 0.0 copy-done
  145.9 0.5 broadcast_select_fusion.1
  146.4 0.7 constant_dynamic-slice_fusion.3
  147.1 0.0 all-gather.19.cloned.1.call-update
  147.2 0.2 all-gather.29.cloned.1.call-start
  147.4 27.5 %all-gather.19.cloned.1.call-done = f32[1024,256]{1,0:T(8,128)} async-done(((f32[256,256]{1,0:T(8,128)}), f32[1024,256]{1,0:T(8,128)}) %all-gather.19.cloned.1.call-update) | async-done | bytes 1048592 | tf_op jit(solution)/shard_map/all_gather | solution.py:32
  174.9 10.1 %fusion.13 = f32[1024,256]{1,0:T(8,128)} fusion(f32[1024,1024]{0,1:T(8,128)} %all-gather.15.cloned.1.call-done, f32[1024,256]{1,0:T(8,128)} %all-gather.19.cloned.1.call-done), kind=kOutput, calls=%fused_computation.37 | convolution fusion | flops 3221225472 | bytes 6291456 | tf_op jit(solution)/shard_map/dot_general | solution.py:39
  185.0 0.0 all-gather.29.cloned.1.call-update
  185.0 0.0 all-gather.23.cloned.1.call-start
  185.1 50.6 %all-gather.29.cloned.1.call-done = f32[4096,256]{1,0:T(8,128)} async-done(((f32[1024,256]{1,0:T(8,128)}), f32[4096,256]{1,0:T(8,128)}) %all-gather.29.cloned.1.call-update) | async-done | bytes 4194320 | tf_op jit(solution)/shard_map/all_gather | solution.py:26
  235.7 2.6 reduce_sum.55
  238.3 0.2 multiply_subtract_fusion.1
  238.5 0.7 constant_dynamic-slice_fusion.1
  239.3 0.0 all-gather.23.cloned.1.call-update
  239.3 0.0 all-gather.21.cloned.1.call-start
  239.3 0.3 copy.5
  239.7 0.7 constant_dynamic-slice_fusion.2
  240.4 0.0 all-gather.21.cloned.1.call-update
  240.4 0.3 all-gather.31.cloned.1.call-start
  240.7 26.3 %all-gather.23.cloned.1.call-done = f32[1024,256]{1,0:T(8,128)} async-done(((f32[256,256]{1,0:T(8,128)}), f32[1024,256]{1,0:T(8,128)}) %all-gather.23.cloned.1.call-update) | async-done | bytes 1048592 | tf_op jit(solution)/shard_map/all_gather | solution.py:32
  267.0 44.9 %all-gather.21.cloned.1.call-done = f32[1024,1024]{0,1:T(8,128)} async-done(((f32[1024,64]{0,1:T(8,128)}), f32[1024,1024]{0,1:T(8,128)}) %all-gather.21.cloned.1.call-update) | async-done | bytes 4194320 | tf_op jit(solution)/shard_map/all_gather | solution.py:40
  311.9 10.1 %fusion.14 = f32[1024,256]{1,0:T(8,128)} fusion(f32[1024,1024]{0,1:T(8,128)} %all-gather.21.cloned.1.call-done, f32[1024,256]{1,0:T(8,128)} %all-gather.23.cloned.1.call-done), kind=kOutput, calls=%fused_computation.38 | convolution fusion | flops 3221225472 | bytes 6291456 | tf_op jit(solution)/shard_map/dot_general | solution.py:39
  322.0 0.0 all-gather.31.cloned.1.call-update
  322.0 0.0 all-gather.25.cloned.1.call-start
  322.1 48.9 %all-gather.31.cloned.1.call-done = f32[4096,256]{1,0:T(8,128)} async-done(((f32[1024,256]{1,0:T(8,128)}), f32[4096,256]{1,0:T(8,128)}) %all-gather.31.cloned.1.call-update) | async-done | bytes 4194320 | tf_op jit(solution)/shard_map/all_gather | solution.py:26
  370.9 2.6 reduce_sum.56
  373.5 0.1 broadcast_select_fusion
  373.6 0.7 constant_dynamic-slice_fusion
  374.4 0.0 all-gather.25.cloned.1.call-update
  374.4 0.3 all-gather.33.cloned.1.call-start
  374.7 27.4 %all-gather.25.cloned.1.call-done = f32[1024,256]{1,0:T(8,128)} async-done(((f32[256,256]{1,0:T(8,128)}), f32[1024,256]{1,0:T(8,128)}) %all-gather.25.cloned.1.call-update) | async-done | bytes 1048592 | tf_op jit(solution)/shard_map/all_gather | solution.py:32
  402.1 10.1 %fusion.15 = f32[1024,256]{1,0:T(8,128)} fusion(f32[1024,1024]{0,1:T(8,128)} %all-gather.21.cloned.1.call-done, f32[1024,256]{1,0:T(8,128)} %all-gather.25.cloned.1.call-done), kind=kOutput, calls=%fused_computation.39 | convolution fusion | flops 3221225472 | bytes 6291456 | tf_op jit(solution)/shard_map/dot_general | solution.py:39
  412.2 0.0 all-gather.33.cloned.1.call-update
  412.3 50.6 %all-gather.33.cloned.1.call-done = f32[4096,256]{1,0:T(8,128)} async-done(((f32[1024,256]{1,0:T(8,128)}), f32[4096,256]{1,0:T(8,128)}) %all-gather.33.cloned.1.call-update) | async-done | bytes 4194320 | tf_op jit(solution)/shard_map/all_gather | solution.py:26
  462.9 2.6 reduce_sum.57
  465.5 2.0 fusion
  467.4 129.7 %all-reduce = (f32[1]{0:T(128)}, f32[1]{0:T(128)}) all-reduce(f32[1]{0:T(128)} %bitcast.17, f32[1]{0:T(128)} %bitcast.16), channel_id=1, replica_groups=mesh['row'=4,'col'=16,'layer'=4] {'row','col'}, use_global_device_ids=true, to_apply=%region_7.8 | all-reduce | flops 2 | bytes 16 | tf_op jit(solution)/shard_map/psum | solution.py:76
  597.1 1.8 pad_maximum_fusion
  (4 shorter events, 0.0 us)
Async XLA Ops:
  7.2 32.2 %all-gather.17.cloned.1.call-start = ((), (), s32[]{:S(2)}) async-start(), calls=%async_computation.1 | async-start | bytes 1310720 | tf_op jit(solution)/shard_map/all_gather | solution.py:32
  8.9 75.3 %all-gather.15.cloned.1.call-start = ((), (), s32[]{:S(2)}) async-start(), calls=%async_computation | async-start | bytes 4456448 | tf_op jit(solution)/shard_map/all_gather | solution.py:40
  11.3 132.0 %all-gather.27.cloned.1.call-start = ((), (), s32[]{:S(2)}) async-start(), calls=%async_computation.6 | async-start | bytes 5242880 | tf_op jit(solution)/shard_map/all_gather | solution.py:26
  94.3 51.5 %copy-start = (s32[64,64]{1,0:T(8,128)S(1)}, s32[64,64]{1,0:T(8,128)}, u32[]{:S(2)}) copy-start(s32[64,64]{1,0:T(8,128)} %param.3) | copy-start | bytes 49156
  94.4 80.5 %all-gather.19.cloned.1.call-start = ((), (), s32[]{:S(2)}) async-start(), calls=%async_computation.2 | async-start | bytes 1310720 | tf_op jit(solution)/shard_map/all_gather | solution.py:32
  147.2 88.5 %all-gather.29.cloned.1.call-start = ((), (), s32[]{:S(2)}) async-start(), calls=%async_computation.7 | async-start | bytes 5242880 | tf_op jit(solution)/shard_map/all_gather | solution.py:26
  185.0 82.0 %all-gather.23.cloned.1.call-start = ((), (), s32[]{:S(2)}) async-start(), calls=%async_computation.4 | async-start | bytes 1310720 | tf_op jit(solution)/shard_map/all_gather | solution.py:32
  239.3 72.6 %all-gather.21.cloned.1.call-start = ((), (), s32[]{:S(2)}) async-start(), calls=%async_computation.3 | async-start | bytes 4456448 | tf_op jit(solution)/shard_map/all_gather | solution.py:40
  240.4 130.5 %all-gather.31.cloned.1.call-start = ((), (), s32[]{:S(2)}) async-start(), calls=%async_computation.8 | async-start | bytes 5242880 | tf_op jit(solution)/shard_map/all_gather | solution.py:26
  322.0 80.1 %all-gather.25.cloned.1.call-start = ((), (), s32[]{:S(2)}) async-start(), calls=%async_computation.5 | async-start | bytes 1310720 | tf_op jit(solution)/shard_map/all_gather | solution.py:32
  374.4 88.5 %all-gather.33.cloned.1.call-start = ((), (), s32[]{:S(2)}) async-start(), calls=%async_computation.9 | async-start | bytes 5242880 | tf_op jit(solution)/shard_map/all_gather | solution.py:26
Sparse Core Ops, SparseCore 0:
  9.8 29.4 all-gather.16
  41.7 42.4 all-gather.14
  94.5 48.7 all-gather.26
  147.3 27.5 all-gather.18
  185.1 50.4 all-gather.28
  239.4 27.5 all-gather.22
  269.4 42.4 all-gather.20
  322.1 48.7 all-gather.30
  374.5 27.5 all-gather.24
  412.4 50.4 all-gather.32
